TPU v7x, 32 devices: a whole 2x2x4 slice. The times are simulated.
32 devices in a mesh: view: 4 (over y, x), tm: 8 (over z, core).
Axes of the slice: x: 2, y: 2, z: 4, core: 2. Of those that a mesh axis runs over, the one named last changes fastest.
Arguments:
- frames: bfloat16 [4, 8192, 768], P('view', 'tm'), may hold values from -100 to 100
- conv_weight: bfloat16 [3, 768, 768], replicated, may hold values from -0.125 to 0.125
- conv_bias: float32 [768], replicated, may hold values from -4 to 4
- proj_weight: bfloat16 [768, 768], replicated, may hold values from -0.21875 to 0.21875
- frames_before: int32 [8192], P('tm'), may hold values from -1 to 1023, as said below
- frames_after: int32 [8192], P('tm'), may hold values from -1 to 1023, as said below
Outputs:
- whitened: float32 [4, 8192, 768], P('view', 'tm')
- pair_loss: float32 [4, 8192], P('view', 'tm')
Inputs may be any that keep to these rules, and one draw needn't show every extreme that they name: Live frames (frames_before >= 0) form clips of consecutive frames, each at most 1024 frames long; inside a clip frames_before counts up from 0 and frames_after counts down to 0; padding frames carry -1 in both lists, and the first and last frames of the timeline are live. `frames_after`: consistent with frames_before, as stated there.
All inputs are finite; a program needn't handle non-finite values.
Results may differ from a plain program's by a relative error of at most 0.0045.
Values may be sent and summed in bfloat16 or wider, within the bound.
A program may use at most 128 MiB of HBM per device.

v0:
```python
import jax
import jax.numpy as jnp
from jax import lax
from jax.sharding import PartitionSpec as P

DILATION_STEP = 4
eps_shrink = 0.001


def padded(shard, sides, width):
    for axis, dim in sides:
        count, length = (lax.axis_size(axis), shard.shape[dim])
        up = [(i, (i + 1) % count) for i in range(count - 1)]
        down = [(j, i) for i, j in up]
        last = lax.slice_in_dim(shard, length - width, length, axis=dim)
        first = lax.slice_in_dim(shard, 0, width, axis=dim)
        before = lax.ppermute(last, axis, up)
        after = lax.ppermute(first, axis, down)
        shard = jnp.concatenate([before, shard, after], axis=dim)
    return shard


def partner_2(value, axis, distance):
    mask = 2**distance
    pairs = [(source, source ^ mask) for source in range(lax.axis_size(axis))]
    return lax.ppermute(value, axis, pairs)


def per_device(frames, conv_weight, conv_bias, proj_weight, frames_before, frames_after):
    local_frames = frames[0]
    frame_rows = local_frames.shape[0]
    width = proj_weight.shape[1]
    live = (frames_before >= 0).astype(jnp.float32)
    padded_input = padded(local_frames, (("tm", 0),), DILATION_STEP)
    total = jnp.zeros((frame_rows, local_frames.shape[1]), jnp.float32)
    for frame_index in range(3):
        shift_amount = (frame_index - 1) * DILATION_STEP
        valid = ((frames_before >= -shift_amount) & (frames_after >= shift_amount)).astype(
            jnp.float32
        )
        shifted_input = padded_input[
            DILATION_STEP + shift_amount : DILATION_STEP + shift_amount + frame_rows
        ]
        term = jnp.dot(shifted_input, conv_weight[frame_index], preferred_element_type=jnp.float32)
        total = total + valid[:, None] * term
    hidden = (live[:, None] * jax.nn.gelu(total + conv_bias[None, :], approximate=True)).astype(
        jnp.bfloat16
    )
    embed = jnp.dot(hidden, proj_weight, preferred_element_type=jnp.float32)
    identity = jnp.eye(width, dtype=jnp.float32)
    count, sums = lax.psum((jnp.sum(live), jnp.sum(embed, axis=0)), "tm")
    mean = sums / count
    centered = live[:, None] * (embed - mean[None, :])
    gram = jnp.dot(
        centered.T, centered, precision=lax.Precision.HIGHEST, preferred_element_type=jnp.float32
    )
    cov = lax.psum(gram, "tm") / count + eps_shrink * identity
    factor = jnp.linalg.cholesky(cov)
    whitened = jax.scipy.linalg.solve_triangular(factor, centered.T, lower=True).T
    partner = partner_2(whitened, "view", 0)
    diff = whitened - partner
    pair_loss = jnp.sum(diff * diff, axis=1) / width
    return (whitened[None], pair_loss[None])


def solution(mesh):
    return jax.shard_map(
        per_device,
        mesh=mesh,
        in_specs=(P("view", "tm", None), P(), P(), P(), P("tm"), P("tm")),
        out_specs=(P("view", "tm", None), P("view", "tm")),
        check_vma=False,
    )
```

profile of v0, /device:TPU:0, one launch (start us, length us, event | category | flops | bytes accessed | tf_op | source)
XLA Modules:
  0.0 508.7 jit_solution(16603744037829397869)
XLA Ops:
  13.7 4.9 fusion.40
  18.6 4.4 fusion.21
  23.1 8.5 %fusion.92 = (f32[768]{0:T(1024)S(1)}, f32[1024,768]{1,0:T(8,128)}) fusion(bf16[768,768]{1,0:T(8,128)(2,1)S(1)} %copy-done, f32[1024,768]{1,0:T(8,128)} %fusion.40, f32[1024,768]{1,0:T(8,128)} %fusion.21, bf16[4,768]{1,0:T(4,128)(2,1)S(1)} %collective-permute-done.1, bf16[1024,768]{1,0:T(8,128)(2,1)S(1)} %bitcast.104, f32[768]{0:T(1024)S(1)} %copy-done.15, ...), kind=kOutput, calls=%fused_computation.161 | convolution fusion | flops 2432433408 | bytes 13398016 | tf_op jit(solution)/shard_map/dot_general | solution.py:49
  31.5 19.0 %all-reduce.1 = (f32[768]{0:T(1024)S(1)}, f32[]{:T(128)}) all-reduce(f32[768]{0:T(1024)S(1)} %get-tuple-element.56, f32[]{:T(128)} %get-tuple-element.26), channel_id=1, replica_groups=mesh['view'=4,'tm'=8] {'tm'}, use_global_device_ids=true, to_apply=%region_1.0 | all-reduce | flops 769 | bytes 6152 | tf_op jit(solution)/shard_map/psum | solution.py:51
  51.2 12.5 %fusion.10 = f32[768,768]{0,1:T(8,128)} fusion(f32[1024,768]{1,0:T(8,128)} %get-tuple-element.57, f32[768]{0:T(1024)S(1)} %broadcast_divide_fusion, f32[1024]{0:T(1024)S(1)} %get-tuple-element.55), kind=kOutput, calls=%fused_computation.15 | convolution fusion | flops 7249330176 | bytes 5512192 | tf_op jit(solution)/shard_map/dot_general | solution.py:54
  64.4 4.1 fusion.9
  68.4 60.5 %all-reduce.4.cloned.1.call-done = f32[768,768]{0,1:T(8,128)} async-done(((f32[768,768]{0,1:T(8,128)}), f32[768,768]{0,1:T(8,128)}) %all-reduce.4.cloned.1.call-update) | async-done | bytes 2359312 | tf_op jit(solution)/shard_map/psum | solution.py:57
  128.9 3.9 select_add_fusion
  140.3 11.7 %cholesky.164 = f32[128,128]{1,0:T(8,128)S(1)} custom-call(f32[128,128]{1,0:T(8,128)S(1)} %cholesky.421), custom_call_target="Cholesky" | custom-call | tf_op jit(solution)/shard_map/jit(cholesky)/cholesky | solution.py:58
  152.7 9.8 %custom-call.47 = f32[1,128,128]{1,2,0:T(8,128)S(1)} custom-call(f32[1,128,128]{2,1,0:T(8,128)S(1)} %get-tuple-element.51), custom_call_target="InvertDiagBlocksLowerTriangular" | custom-call | tf_op jit(solution)/shard_map/jit(cholesky)/cholesky | solution.py:58
  166.3 11.7 %cholesky.187 = f32[128,128]{1,0:T(8,128)S(1)} custom-call(f32[128,128]{1,0:T(8,128)S(1)} %cholesky.425), custom_call_target="Cholesky" | custom-call | tf_op jit(solution)/shard_map/jit(cholesky)/cholesky | solution.py:58
  178.7 10.6 %custom-call.48 = f32[1,128,128]{1,2,0:T(8,128)} custom-call(f32[1,128,128]{2,1,0:T(8,128)S(1)} %get-tuple-element.49), custom_call_target="InvertDiagBlocksLowerTriangular" | custom-call | tf_op jit(solution)/shard_map/jit(cholesky)/cholesky | solution.py:58
  194.2 13.2 %cholesky.352 = f32[128,128]{1,0:T(8,128)} custom-call(f32[128,128]{1,0:T(8,128)} %cholesky.430), custom_call_target="Cholesky" | custom-call | tf_op jit(solution)/shard_map/jit(cholesky)/cholesky | solution.py:58
  211.2 11.3 %custom-call.49 = f32[1,128,128]{1,2,0:T(8,128)} custom-call(f32[1,128,128]{2,1,0:T(8,128)} %get-tuple-element.47), custom_call_target="InvertDiagBlocksLowerTriangular" | custom-call | tf_op jit(solution)/shard_map/jit(cholesky)/cholesky | solution.py:58
  227.2 13.6 %cholesky.371 = f32[128,128]{1,0:T(8,128)} custom-call(f32[128,128]{1,0:T(8,128)} %cholesky.435), custom_call_target="Cholesky" | custom-call | tf_op jit(solution)/shard_map/jit(cholesky)/cholesky | solution.py:58
  244.6 11.3 %custom-call.50 = f32[1,128,128]{1,2,0:T(8,128)} custom-call(f32[1,128,128]{2,1,0:T(8,128)} %get-tuple-element.45), custom_call_target="InvertDiagBlocksLowerTriangular" | custom-call | tf_op jit(solution)/shard_map/jit(cholesky)/cholesky | solution.py:58
  260.3 13.2 %cholesky.390 = f32[128,128]{1,0:T(8,128)} custom-call(f32[128,128]{1,0:T(8,128)} %cholesky.440), custom_call_target="Cholesky" | custom-call | tf_op jit(solution)/shard_map/jit(cholesky)/cholesky | solution.py:58
  277.9 11.3 %custom-call.51 = f32[1,128,128]{1,2,0:T(8,128)} custom-call(f32[1,128,128]{2,1,0:T(8,128)} %get-tuple-element.43), custom_call_target="InvertDiagBlocksLowerTriangular" | custom-call | tf_op jit(solution)/shard_map/jit(cholesky)/cholesky | solution.py:58
  292.6 13.2 %cholesky.408 = f32[128,128]{1,0:T(8,128)} custom-call(f32[128,128]{1,0:T(8,128)} %convolution_subtract_fusion.7), custom_call_target="Cholesky" | custom-call | tf_op jit(solution)/shard_map/jit(cholesky)/cholesky | solution.py:58
  319.7 21.0 %while.1 = (s32[]{:T(128)}, f32[768,768]{0,1:T(8,128)}, s32[6,2]{0,1:T(2,128)S(1)}, f32[6,128,128]{2,1,0:T(8,128)}, s32[]{:T(128)}) while((s32[]{:T(128)}, f32[768,768]{0,1:T(8,128)}, s32[6,2]{0,1:T(2,128)S(1)}, f32[6,128,128]{2,1,0:T(8,128)}, s32[]{:T(128)}) %tuple.46), condition=%wide.while_cond, body=%wide.while_body.sunk | while | flops 2 | bytes 393329 | solution.py:59
  340.7 60.0 %custom-call.52 = f32[6,128,128]{1,2,0:T(8,128)S(1)} custom-call(f32[6,128,128]{2,1,0:T(8,128)} %get-tuple-element.9), custom_call_target="InvertDiagBlocksLowerTriangular" | custom-call | tf_op jit(solution)/shard_map/jit(_solve_triangular)/triangular_solve | solution.py:59
  416.4 4.4 fusion.34
  422.3 5.6 %convolution_subtract_fusion.1 = f32[128,1024]{0,1:T(8,128)S(1)} fusion(f32[640,1024]{1,0:T(8,128)S(1)} %get-tuple-element.32, f32[768,1024]{0,1:T(8,128)S(1)} %copy-done.1, f32[768,768]{0,1:T(8,128)} %get-tuple-element.110), kind=kOutput, calls=%fused_computation.47 | convolution fusion | flops 1006764032 | bytes 3997696 | tf_op jit(solution)/shard_map/jit(_solve_triangular)/triangular_solve | solution.py:59
  434.5 63.2 %collective-permute-done.2 = f32[1024,768]{0,1:T(8,128)} collective-permute-done((f32[1024,768]{0,1:T(8,128)}, f32[1024,768]{0,1:T(8,128)}, u32[]{:S(2)}, u32[]{:S(2)}) %collective-permute-start.2) | collective-permute-done | bytes 3145760 | tf_op jit(solution)/shard_map/ppermute | solution.py:26
  (133 shorter events, 108.4 us)
Async XLA Ops:
  7.2 15.9 %copy-start = (bf16[768,768]{1,0:T(8,128)(2,1)S(1)}, bf16[768,768]{1,0:T(8,128)(2,1)}, u32[]{:S(2)}) copy-start(bf16[768,768]{1,0:T(8,128)(2,1)} %param.9) | copy-start | bytes 3538948
  7.2 121.8 %all-reduce.4.cloned.1.call-start = ((), (), s32[]{:S(2)}) async-start(), calls=%async_computation | async-start | bytes 4718592 | tf_op jit(solution)/shard_map/psum | solution.py:57
  8.0 15.0 %collective-permute-start.1 = (bf16[4,768]{1,0:T(4,128)(2,1)S(1)}, bf16[4,768]{1,0:T(4,128)(2,1)S(1)}, u32[]{:S(2)}, u32[]{:S(2)}) collective-permute-start(bf16[4,768]{1,0:T(4,128)(2,1)S(1)} %get-tuple-element.30), channel_id=1, source_target_pairs={{1,0},{2,1},{3,2},{4,3},{5,4},{6,5},{7,6},{9,8},{10,9},{11,10},{12... | collective-permute-start | bytes 18440 | tf_op jit(solution)/shard_map/ppermute | solution.py:18
  9.3 9.3 %collective-permute-start = (bf16[4,768]{1,0:T(4,128)(2,1)S(1)}, bf16[4,768]{1,0:T(4,128)(2,1)S(1)}, u32[]{:S(2)}, u32[]{:S(2)}) collective-permute-start(bf16[4,768]{1,0:T(4,128)(2,1)S(1)} %get-tuple-element.31), channel_id=1, source_target_pairs={{0,1},{1,2},{2,3},{3,4},{4,5},{5,6},{6,7},{8,9},{9,10},{10,11},{11... | collective-permute-start | bytes 18440 | tf_op jit(solution)/shard_map/ppermute | solution.py:17
  13.7 4.9 copy-start.12
  13.7 4.9 copy-start.13
  13.7 4.9 copy-start.14
  18.6 4.4 copy-start.15
  132.8 3.4 copy-start.2
  138.9 1.4 copy-start.3
  165.4 13.4 %copy-start.4 = (f32[640,128]{1,0:T(8,128)}, f32[640,128]{1,0:T(8,128)S(1)}, u32[]{:S(2)}) copy-start(f32[640,128]{1,0:T(8,128)S(1)} %convolution_subtract_fusion.3) | copy-start | bytes 983044
  189.4 1.1 copy-start.6
  189.4 1.1 copy-start.10
  189.4 1.1 copy-start.5
  189.4 1.2 copy-start.11
  192.9 0.7 copy-start.7
  225.9 0.7 copy-start.8
  259.0 0.6 copy-start.9
  318.0 1.6 copy-start.16
  403.2 3.7 copy-start.1
  429.4 68.3 %collective-permute-start.2 = (f32[1024,768]{0,1:T(8,128)}, f32[1024,768]{0,1:T(8,128)}, u32[]{:S(2)}, u32[]{:S(2)}) collective-permute-start(f32[1024,768]{0,1:T(8,128)} %bitcast.24), channel_id=1, source_target_pairs={{0,8},{8,0},{16,24},{24,16},{1,9},{9,1},{17,25},{25,17},{2,10},{10... | collective-permute-start | bytes 9437192 | tf_op jit(solution)/shard_map/ppermute | solution.py:26
Sparse Core Ops, SparseCore 0:
  63.9 65.0 all-reduce.3
where the time goes:
time: 515 us; the launch traced here: 509 us
  other arithmetic  220 us (43%)
  waiting for transfers between devices  124 us (24%)
  matrix products  74.2 us (14%)
  local copies, waits for them, and re-layouts  47.1 us (9%)
  blocking collectives  19 us (4%)
  between operations  18.5 us (4%)
  starting transfers between devices  5.82 us (1%)
    another operation x22, other arithmetic, per_device(): factor = jnp.linalg.cholesky(cov)  142 us
    ppermute x1, waiting for transfers between devices, partner_2(): return lax.ppermute(value, axis, pairs)  63.2 us
    another operation x3, other arithmetic, per_device(): jax.scipy.linalg.solve_triangular(factor, centered.T, lower=True)  62.2 us
    psum x1, waiting for transfers between devices, per_device(): cov = lax.psum(gram, 'tm') / count + eps_shrink * identity  60.5 us
    another operation x11, matrix products, per_device(): jax.scipy.linalg.solve_triangular(factor, centered.T, lower=True)  28.7 us
    another operation x30, local copies, waits for them, and re-layouts  20.9 us
    psum x1, blocking collectives, per_device(): count, sums = lax.psum((jnp.sum(live), jnp.sum(embed, axis=0)), 'tm')  19 us
    another operation x10, matrix products, per_device(): factor = jnp.linalg.cholesky(cov)  15.2 us
  transfers between devices with their start and end apart: 4, of which 2 were waited for; matrix products, arithmetic and copies ran while one was open for 4% of the time, Pallas kernels for 0%

commit v1 on v0

--- a/solution.py
+++ b/solution.py
@@ -54,7 +54,7 @@
     gram = jnp.dot(
         centered.T, centered, precision=lax.Precision.HIGHEST, preferred_element_type=jnp.float32
     )
-    cov = lax.psum(gram, "tm") / count + eps_shrink * identity
+    cov = jnp.sum(lax.all_gather(gram, "tm"), axis=0) / count + eps_shrink * identity
     factor = jnp.linalg.cholesky(cov)
     whitened = jax.scipy.linalg.solve_triangular(factor, centered.T, lower=True).T
     partner = partner_2(whitened, "view", 0)

time: 515 us -> 580 us (1.13)
  waiting for transfers between devices: 124 us -> 228 us
  local copies, waits for them, and re-layouts: 47.1 us -> 27.3 us
  other arithmetic: 220 us -> 206 us
    all_gather x0 -> x1, waiting for transfers between devices: none -> 163 us  [per_device(): lax.all_gather(gram, 'tm')]
    psum x1 -> x0, waiting for transfers between devices: 60.5 us -> none  [per_device(): cov = lax.psum(gram, 'tm') / count + eps_shrink * identity]
    another operation x22, other arithmetic: 142 us -> 124 us  [per_device(): factor = jnp.linalg.cholesky(cov)]
    another operation x19 -> x6, local copies, waits for them, and re-layouts: 14.9 us -> 0.19 us  [per_device(): factor = jnp.linalg.cholesky(cov)]
    reduce_sum x0 -> x1, other arithmetic: none -> 7.87 us  [per_device(): jnp.sum(lax.all_gather(gram, 'tm'), axis=0) / count + eps_shrink * identity]
    another operation x30 -> x18, local copies, waits for them, and re-layouts: 20.9 us -> 18 us
  transfers between devices with their start and end apart: 4 -> 4, of which waited for: 2 -> 2; matrix products, arithmetic and copies ran while one was open for 4% -> 3% of each run, Pallas kernels for 0% -> 0%
where the time goes in v1:
time: 580 us; the launch traced here: 574 us
  waiting for transfers between devices  228 us (39%)
  other arithmetic  206 us (36%)
  matrix products  68.7 us (12%)
  local copies, waits for them, and re-layouts  27.3 us (5%)
  blocking collectives  20 us (3%)
  between operations  18.6 us (3%)
    all_gather x1, waiting for transfers between devices, per_device(): lax.all_gather(gram, 'tm')  163 us
    another operation x22, other arithmetic, per_device(): factor = jnp.linalg.cholesky(cov)  124 us
    ppermute x1, waiting for transfers between devices, partner_2(): return lax.ppermute(value, axis, pairs)  65.5 us
    another operation x3, other arithmetic, per_device(): jax.scipy.linalg.solve_triangular(factor, centered.T, lower=True)  60.6 us
    another operation x11, matrix products, per_device(): jax.scipy.linalg.solve_triangular(factor, centered.T, lower=True)  28.6 us
    psum x1, blocking collectives, per_device(): count, sums = lax.psum((jnp.sum(live), jnp.sum(embed, axis=0)), 'tm')  20 us
    another operation x18, local copies, waits for them, and re-layouts  18 us
    dot_general x1, matrix products, per_device(): jnp.dot(centered.T, centered, precision=lax.Precision.HIGHEST, preferred_...  12.6 us
  transfers between devices with their start and end apart: 4, of which 2 were waited for; matrix products, arithmetic and copies ran while one was open for 3% of the time, Pallas kernels for 0%

profile of v1, /device:TPU:0, one launch (start us, length us, event | category | flops | bytes accessed | tf_op | source)
XLA Modules:
  0.0 574.1 jit_solution(5190583398340691572)
XLA Ops:
  11.9 4.8 fusion.39
  17.3 4.4 fusion.20
  21.7 8.5 %fusion.92 = (f32[768]{0:T(1024)S(1)}, f32[1024,768]{1,0:T(8,128)}) fusion(bf16[768,768]{1,0:T(8,128)(2,1)S(1)} %copy-done, f32[1024,768]{1,0:T(8,128)} %fusion.39, f32[1024,768]{1,0:T(8,128)} %fusion.20, bf16[4,768]{1,0:T(4,128)(2,1)S(1)} %collective-permute-done.1, bf16[1024,768]{1,0:T(8,128)(2,1)S(1)} %bitcast.106, f32[768]{0:T(1024)S(1)} %copy-done.7, ...), kind=kOutput, calls=%fused_computation.162 | convolution fusion | flops 2432433408 | bytes 13398016 | tf_op jit(solution)/shard_map/dot_general | solution.py:49
  30.2 20.0 %all-reduce.1 = (f32[768]{0:T(1024)S(1)}, f32[]{:T(128)}) all-reduce(f32[768]{0:T(1024)S(1)} %get-tuple-element.58, f32[]{:T(128)} %get-tuple-element.22), channel_id=1, replica_groups=mesh['view'=4,'tm'=8] {'tm'}, use_global_device_ids=true, to_apply=%region_1.0 | all-reduce | flops 769 | bytes 6152 | tf_op jit(solution)/shard_map/psum | solution.py:51
  50.8 12.6 %fusion.10 = f32[768,768]{1,0:T(8,128)} fusion(f32[1024,768]{1,0:T(8,128)} %get-tuple-element.59, f32[768]{0:T(1024)S(1)} %broadcast_divide_fusion.1, f32[1024]{0:T(1024)S(1)} %get-tuple-element.57), kind=kOutput, calls=%fused_computation.15 | convolution fusion | flops 7249330176 | bytes 5512192 | tf_op jit(solution)/shard_map/dot_general | solution.py:54
  63.4 4.1 fusion.9
  67.5 162.6 %all-gather.3.cloned.1.call-done = f32[6144,768]{1,0:T(8,128)} async-done(((f32[768,768]{1,0:T(8,128)}), f32[6144,768]{1,0:T(8,128)}) %all-gather.3.cloned.1.call-update) | async-done | bytes 18874384 | tf_op jit(solution)/shard_map/all_gather | solution.py:57
  230.1 7.9 %reduce_sum.38 = f32[768,768]{1,0:T(8,128)S(1)} reduce(f32[8,768,768]{2,1,0:T(8,128)} %bitcast.103, f32[]{:T(128)} %constant.221.clone.1), dimensions={0}, to_apply=%region_4.0 | reduce | flops 4128768 | bytes 21233668 | tf_op jit(solution)/shard_map/reduce_sum | solution.py:57
  247.5 11.7 %cholesky.164 = f32[128,128]{1,0:T(8,128)S(1)} custom-call(f32[128,128]{1,0:T(8,128)S(1)} %cholesky.421), custom_call_target="Cholesky" | custom-call | tf_op jit(solution)/shard_map/jit(cholesky)/cholesky | solution.py:58
  259.4 9.8 %custom-call.47 = f32[1,128,128]{1,2,0:T(8,128)S(1)} custom-call(f32[1,128,128]{2,1,0:T(8,128)S(1)} %get-tuple-element.53), custom_call_target="InvertDiagBlocksLowerTriangular" | custom-call | tf_op jit(solution)/shard_map/jit(cholesky)/cholesky | solution.py:58
  272.0 11.7 %cholesky.187 = f32[128,128]{1,0:T(8,128)S(1)} custom-call(f32[128,128]{1,0:T(8,128)S(1)} %cholesky.425), custom_call_target="Cholesky" | custom-call | tf_op jit(solution)/shard_map/jit(cholesky)/cholesky | solution.py:58
  283.7 10.2 %custom-call.48 = f32[1,128,128]{1,2,0:T(8,128)S(1)} custom-call(f32[1,128,128]{2,1,0:T(8,128)S(1)} %get-tuple-element.50), custom_call_target="InvertDiagBlocksLowerTriangular" | custom-call | tf_op jit(solution)/shard_map/jit(cholesky)/cholesky | solution.py:58
  295.9 11.7 %cholesky.352 = f32[128,128]{1,0:T(8,128)S(1)} custom-call(f32[128,128]{1,0:T(8,128)S(1)} %cholesky.430), custom_call_target="Cholesky" | custom-call | tf_op jit(solution)/shard_map/jit(cholesky)/cholesky | solution.py:58
  307.6 9.8 %custom-call.49 = f32[1,128,128]{1,2,0:T(8,128)S(1)} custom-call(f32[1,128,128]{2,1,0:T(8,128)S(1)} %get-tuple-element.47), custom_call_target="InvertDiagBlocksLowerTriangular" | custom-call | tf_op jit(solution)/shard_map/jit(cholesky)/cholesky | solution.py:58
  319.3 11.8 %cholesky.371 = f32[128,128]{1,0:T(8,128)S(1)} custom-call(f32[128,128]{1,0:T(8,128)S(1)} %cholesky.435), custom_call_target="Cholesky" | custom-call | tf_op jit(solution)/shard_map/jit(cholesky)/cholesky | solution.py:58
  331.2 9.8 %custom-call.50 = f32[1,128,128]{1,2,0:T(8,128)S(1)} custom-call(f32[1,128,128]{2,1,0:T(8,128)S(1)} %get-tuple-element.44), custom_call_target="InvertDiagBlocksLowerTriangular" | custom-call | tf_op jit(solution)/shard_map/jit(cholesky)/cholesky | solution.py:58
  342.8 11.7 %cholesky.390 = f32[128,128]{1,0:T(8,128)S(1)} custom-call(f32[128,128]{1,0:T(8,128)S(1)} %cholesky.440), custom_call_target="Cholesky" | custom-call | tf_op jit(solution)/shard_map/jit(cholesky)/cholesky | solution.py:58
  354.5 9.8 %custom-call.51 = f32[1,128,128]{1,2,0:T(8,128)S(1)} custom-call(f32[1,128,128]{2,1,0:T(8,128)S(1)} %get-tuple-element.41), custom_call_target="InvertDiagBlocksLowerTriangular" | custom-call | tf_op jit(solution)/shard_map/jit(cholesky)/cholesky | solution.py:58
  365.9 11.9 %cholesky.408 = f32[128,128]{1,0:T(8,128)S(1)} custom-call(f32[128,128]{1,0:T(8,128)S(1)} %convolution_subtract_fusion.7), custom_call_target="Cholesky" | custom-call | tf_op jit(solution)/shard_map/jit(cholesky)/cholesky | solution.py:58
  386.6 18.1 %while.1 = (s32[]{:T(128)}, f32[768,768]{1,0:T(8,128)}, s32[6,2]{0,1:T(2,128)S(1)}, f32[6,128,128]{2,1,0:T(8,128)S(1)}, s32[]{:T(128)}) while((s32[]{:T(128)}, f32[768,768]{1,0:T(8,128)}, s32[6,2]{0,1:T(2,128)S(1)}, f32[6,128,128]{2,1,0:T(8,128)S(1)}, s32[]{:T(128)}) %tuple.51), condition=%wide.while_cond, body=%wide.while_body.sunk | while | flops 2 | bytes 131189 | solution.py:59
  404.7 59.0 %custom-call.52 = f32[6,128,128]{1,2,0:T(8,128)S(1)} custom-call(f32[6,128,128]{2,1,0:T(8,128)S(1)} %get-tuple-element.9), custom_call_target="InvertDiagBlocksLowerTriangular" | custom-call | tf_op jit(solution)/shard_map/jit(_solve_triangular)/triangular_solve | solution.py:59
  479.3 4.4 fusion.33
  485.1 5.7 convolution_subtract_fusion.1
  497.4 65.5 %collective-permute-done.2 = f32[1024,768]{0,1:T(8,128)} collective-permute-done((f32[1024,768]{0,1:T(8,128)}, f32[1024,768]{0,1:T(8,128)}, u32[]{:S(2)}, u32[]{:S(2)}) %collective-permute-start.2) | collective-permute-done | bytes 3145760 | tf_op jit(solution)/shard_map/ppermute | solution.py:26
  (91 shorter events, 76.2 us)
Async XLA Ops:
  7.2 14.5 %copy-start = (bf16[768,768]{1,0:T(8,128)(2,1)S(1)}, bf16[768,768]{1,0:T(8,128)(2,1)}, u32[]{:S(2)}) copy-start(bf16[768,768]{1,0:T(8,128)(2,1)} %param.9) | copy-start | bytes 3538948
  7.2 222.9 %all-gather.3.cloned.1.call-start = ((), (), s32[]{:S(2)}) async-start(), calls=%async_computation | async-start | bytes 21233664 | tf_op jit(solution)/shard_map/all_gather | solution.py:57
  8.0 9.2 %collective-permute-start = (bf16[4,768]{1,0:T(4,128)(2,1)S(1)}, bf16[4,768]{1,0:T(4,128)(2,1)S(1)}, u32[]{:S(2)}, u32[]{:S(2)}) collective-permute-start(bf16[4,768]{1,0:T(4,128)(2,1)S(1)} %get-tuple-element.27), channel_id=1, source_target_pairs={{0,1},{1,2},{2,3},{3,4},{4,5},{5,6},{6,7},{8,9},{9,10},{10,11},{11... | collective-permute-start | bytes 18440 | tf_op jit(solution)/shard_map/ppermute | solution.py:17
  10.4 6.3 %copy-start.4 = (s32[1024]{0:T(1024)S(1)}, s32[1024]{0:T(1024)}, u32[]{:S(2)}) copy-start(s32[1024]{0:T(1024)} %param.10) | copy-start | bytes 12292
  10.4 6.9 %copy-start.5 = (s32[1024]{0:T(1024)S(1)}, s32[1024]{0:T(1024)}, u32[]{:S(2)}) copy-start(s32[1024]{0:T(1024)} %param.11) | copy-start | bytes 12292
  10.4 6.9 %copy-start.6 = (bf16[1,1024,768]{2,1,0:T(8,128)(2,1)S(1)}, bf16[1,1024,768]{2,1,0:T(8,128)(2,1)}, u32[]{:S(2)}) copy-start(bf16[1,1024,768]{2,1,0:T(8,128)(2,1)} %param.6) | copy-start | bytes 4718596
  10.4 11.2 %collective-permute-start.1 = (bf16[4,768]{1,0:T(4,128)(2,1)S(1)}, bf16[4,768]{1,0:T(4,128)(2,1)S(1)}, u32[]{:S(2)}, u32[]{:S(2)}) collective-permute-start(bf16[4,768]{1,0:T(4,128)(2,1)S(1)} %get-tuple-element.26), channel_id=1, source_target_pairs={{1,0},{2,1},{3,2},{4,3},{5,4},{6,5},{7,6},{9,8},{10,9},{11,10},{12... | collective-permute-start | bytes 18440 | tf_op jit(solution)/shard_map/ppermute | solution.py:18
  17.3 4.4 copy-start.7
  246.0 1.4 copy-start.3
  466.1 3.7 copy-start.2
  492.3 70.6 %collective-permute-start.2 = (f32[1024,768]{0,1:T(8,128)}, f32[1024,768]{0,1:T(8,128)}, u32[]{:S(2)}, u32[]{:S(2)}) collective-permute-start(f32[1024,768]{0,1:T(8,128)} %bitcast.25), channel_id=1, source_target_pairs={{0,8},{8,0},{16,24},{24,16},{1,9},{9,1},{17,25},{25,17},{2,10},{10... | collective-permute-start | bytes 9437192 | tf_op jit(solution)/shard_map/ppermute | solution.py:26
  493.8 73.1 %copy-start.1 = (bf16[768,768]{1,0:T(8,128)(2,1)S(1)}, bf16[768,768]{1,0:T(8,128)(2,1)}, u32[]{:S(2)}) copy-start(bf16[768,768]{1,0:T(8,128)(2,1)} %param.9) | copy-start | bytes 3538948
Sparse Core Ops, SparseCore 0:
  63.5 166.4 all-gather.2
